TPU v7x, 32 devices: a whole 2x2x4 slice. The times are simulated.
32 devices in a mesh: section: 4 (over y, x), tile: 8 (over z, core).
Axes of the slice: x: 2, y: 2, z: 4, core: 2. Of those that a mesh axis runs over, the one named last changes fastest.
Arguments:
- carried_act: bfloat16 [4, 48, 16, 16, 256], P('section', 'tile'), may hold values from -6 to 6
- stored_out: bfloat16 [4, 48, 16, 16, 256], P('section', 'tile'), may hold values from -6 to 6
- cotangent: bfloat16 [4, 48, 16, 16, 256], P('section', 'tile'), may hold values from -6 to 6
- weights: bfloat16 [4, 2, 27, 128, 128], P('section'), may hold values from -0.109375 to 0.109375
- momentum: float32 [4, 2, 27, 128, 128], P('section'), may hold values from -6 to 6
Outputs:
- forward_out: bfloat16 [4, 48, 16, 16, 256], P('section', 'tile')
- input_grad: bfloat16 [4, 48, 16, 16, 256], P('section', 'tile')
- new_momentum: float32 [4, 2, 27, 128, 128], P('section')
All inputs are finite; a program needn't handle non-finite values.
Results may differ from a plain program's by a relative error of at most 0.006.
Values may be sent and summed in bfloat16 or wider, within the bound.
A program may use at most 128 MiB of HBM per device.

v0:
```python
import functools

import jax
import jax.numpy as jnp
from jax import lax
from jax.experimental import pallas as pl
from jax.experimental.pallas import tpu as pltpu
from jax.sharding import PartitionSpec as P

momentum_decay = 0.9
grad_weight = 0.25
BF = jnp.bfloat16
F32 = jnp.float32


def kernel(
    ns, nt, tp, step,
    act, stored, cot, w,
    fwd, igrad, gsum,
    xz, xr, xpg, xpf, xa, xb, halo, a_in, c_in, gz_s, fz_s, wt, pg_s, pf_s,
    grad, got1, part, got2, total, send, recv,
):
    depth, hy, wx = a_in.shape[1:4]
    half = w.shape[-1]
    s = lax.axis_index("section")
    t = lax.axis_index("tile")
    m = nt // 2
    chip, core = t // 2, lax.rem(t, 2)
    partner = 2 * chip + (1 - core)
    nxt, prv = lax.rem(s + 1, ns), lax.rem(s + ns - 1, ns)
    has_low, has_high = t > 0, t < nt - 1
    plane = hy * wx
    rows = step * plane
    steps = depth // step
    used = [0]

    def at(sec, tile):
        return {"section": sec, "tile": tile}

    def copy(src, dst, sec, tile):
        i = used[0]
        used[0] += 1
        return pltpu.make_async_remote_copy(
            src_ref=src, dst_ref=dst, send_sem=send.at[i], recv_sem=recv.at[i],
            device_id=at(sec, tile), device_id_type=pl.DeviceIdType.MESH,
        )

    barrier = pltpu.get_barrier_semaphore()

    def hail(sec, tile):
        pl.semaphore_signal(
            barrier, inc=1, device_id=at(sec, tile), device_id_type=pl.DeviceIdType.MESH
        )

    hail(nxt, t)
    hail(prv, t)
    for d in range(1, m):
        hail(s, lax.rem(t + 2 * d, nt))

    hail(s, lax.rem(t + 1, nt))
    hail(s, lax.rem(t + nt - 1, nt))
    pl.semaphore_wait(barrier, m + 3)

    def mid(x, z):
        return x.at[z, pl.ds(1, hy), :, pl.ds(half, half)]

    def halo_copies(slot, first, last):
        down = copy(first, halo.at[slot, 1], s, lax.rem(t + nt - 1, nt))
        up = copy(last, halo.at[slot, 0], s, lax.rem(t + 1, nt))
        return down, up

    def halo_start(pair):
        @pl.when(has_low)
        def _():
            pair[0].start()

        @pl.when(has_high)
        def _():
            pair[1].start()

    def fill(x, z, count, value):
        n = count * plane
        value = value.reshape(n, half)
        col = lax.rem(lax.broadcasted_iota(jnp.int32, (n, half), 0), wx)
        left = jnp.where(col == 0, 0.0, pltpu.roll(value, 1, 0))
        right = jnp.where(col == wx - 1, 0.0, pltpu.roll(value, n - 1, 0))
        for k, v in enumerate((left, value, right)):
            x[pl.ds(z, count), pl.ds(1, hy), :, pl.ds(k * half, half)] = (
                v.astype(BF).reshape(count, hy, wx, half)
            )

    def halo_finish(pair, slot, x):
        @pl.when(has_low)
        def _():
            pair[0].wait_send()
            pair[1].wait_recv()
            fill(x, 0, 1, halo[slot, 0].astype(F32))

        @pl.when(has_high)
        def _():
            pair[1].wait_send()
            pair[0].wait_recv()
            fill(x, depth + 1, 1, halo[slot, 1].astype(F32))

    def clear(x):
        edge = jnp.zeros((depth + 2, 1, wx, 3 * half), BF)
        x[:, pl.ds(0, 1)] = edge
        x[:, pl.ds(hy + 1, 1)] = edge
        empty = jnp.zeros((1, hy, wx, 3 * half), BF)

        @pl.when(t == 0)
        def _():
            x[pl.ds(0, 1), pl.ds(1, hy)] = empty

        @pl.when(t == nt - 1)
        def _():
            x[pl.ds(depth + 1, 1), pl.ds(1, hy)] = empty

    def conv(x, weight, z):
        cols = jnp.concatenate(
            [
                x[pl.ds(z + i, step), pl.ds(j, hy)].reshape(rows, 3 * half)
                for i in range(3)
                for j in range(3)
            ],
            axis=1,
        )
        return jnp.dot(cols, weight, preferred_element_type=F32)

    def block(ref, z, part_at, *lead):
        return ref[(*lead, pl.ds(z, step), slice(None), slice(None), pl.ds(part_at * half, half))].astype(
            F32
        ).reshape(rows, half)

    def put(ref, z, part_at, value):
        ref[pl.ds(z, step), :, :, pl.ds(part_at * half, half)] = value.astype(BF).reshape(
            step, hy, wx, half
        )

    def each(body):
        def run(n, carry):
            body(n * step)
            return carry

        lax.fori_loop(0, steps, run, 0)

    z_halo = halo_copies(
        0, stored.at[0, 0, :, :, pl.ds(0, half)], stored.at[0, depth - 1, :, :, pl.ds(0, half)]
    )
    halo_start(z_halo)
    parts = {}
    for name, src, dst, target, piece in (
        ("c2", cot, c_in, prv, 1),
        ("c1", cot, c_in, prv, 0),
        ("a2", act, a_in, nxt, 1),
        ("a1", act, a_in, nxt, 0),
    ):
        view = (0, slice(None), slice(None), slice(None), pl.ds(piece * half, half))
        parts[name] = copy(src.at[view], dst.at[view], target, t)
        parts[name].start()

    for x in (xz, xr, xpg, xpf, xa, xb):
        clear(x)
    each(lambda z: fill(xz, z + 1, step, block(stored, z, 0, 0)))

    def turn(n, carry):
        for which in range(2):
            wt[which, n] = w[0, which, 26 - n].T
        return carry

    lax.fori_loop(0, 27, turn, 0)
    halo_finish(z_halo, 0, xz)

    def flat(ref, *lead):
        return ref[lead].reshape(27 * half, half)

    def reconstruct(z):
        g = jnp.tanh(conv(xz, flat(w, 0, 1), z))
        gz_s[pl.ds(z, step)] = (1.0 - g * g).reshape(step, plane, half)
        fill(xr, z + 1, step, block(stored, z, 1, 0) - g)

    each(reconstruct)
    r_halo = halo_copies(1, mid(xr, 1), mid(xr, depth))
    halo_start(r_halo)
    parts["c2"].wait()

    def pre_g(z):
        v = block(c_in, z, 1, 0) * gz_s[pl.ds(z, step)].reshape(rows, half)
        pg_s[pl.ds(z, step)] = v.astype(BF).reshape(step, plane, half)
        fill(xpg, z + 1, step, v)

    each(pre_g)
    pg_halo = halo_copies(2, mid(xpg, 1), mid(xpg, depth))
    halo_start(pg_halo)

    def wgrad(x, d_ref, g):
        turned = d_ref[...].reshape(depth * plane, half).T
        per = nt // 8
        for share in range(nt):
            for tap in range((share % per) * tp, (share % per + 1) * tp):
                if tap >= 27:
                    grad[g, share // 2, share % 2, tap % tp] = jnp.zeros((16, half), BF)
        for i in range(3):
            cols = jnp.concatenate(
                [
                    x[pl.ds(i, depth), pl.ds(j, hy)].reshape(depth * plane, 3 * half)
                    for j in range(3)
                ],
                axis=1,
            )
            out = jnp.dot(turned, cols, preferred_element_type=F32)
            for q in range(9):
                tap = 9 * i + q
                tile = out[:, q * half : (q + 1) * half].T.astype(BF)
                for r in range(8):
                    share = r * per + tap // tp
                    grad[g, share // 2, share % 2, tap % tp] = tile[16 * r : 16 * (r + 1)]

    def level_1(g):
        c = copy(grad.at[g, :, 1 - core], got1.at[g], s, partner)
        c.start()
        return c

    def level_2(g, c):
        c.wait()
        part[g] = (grad[g, :, core].astype(F32) + got1[g].astype(F32)).astype(BF)
        out = []
        for d in range(1, m):
            to = lax.rem(chip + d, m)
            k = copy(part.at[g, to], got2.at[g, d - 1], s, 2 * to + core)
            k.start()
            out.append(k)
        return out

    def level_3(g, cs):
        for c in cs:
            c.wait()
        acc = part[g, chip].astype(F32)
        for d in range(1, m):
            acc = acc + got2[g, d - 1].astype(F32)
        total[g, chip, core] = acc.astype(BF)
        out = []
        for d in range(1, m):
            to = lax.rem(chip + d, m)
            k = copy(total.at[g, chip, core], total.at[g, chip, core], s, 2 * to + core)
            k.start()
            out.append(k)
        return out

    def level_4(g, cs):
        for c in cs:
            c.wait()
        k = copy(total.at[g, :, core], total.at[g, :, core], s, partner)
        k.start()
        return k

    wgrad(xz, pg_s, 1)
    g1 = level_1(1)
    halo_finish(r_halo, 1, xr)

    def recompute_f(z):
        f = jnp.tanh(conv(xr, flat(w, 0, 0), z))
        fz_s[pl.ds(z, step)] = (1.0 - f * f).reshape(step, plane, half)

    each(recompute_f)
    g2 = level_2(1, g1)
    halo_finish(pg_halo, 2, xpg)
    parts["c1"].wait()

    def grad_one(z):
        d1 = (block(c_in, z, 0, 0) + conv(xpg, flat(wt, 1), z)).astype(BF)
        put(igrad, z, 0, d1)
        v = d1.astype(F32) * fz_s[pl.ds(z, step)].reshape(rows, half)
        pf_s[pl.ds(z, step)] = v.astype(BF).reshape(step, plane, half)
        fill(xpf, z + 1, step, v)

    each(grad_one)
    pf_halo = halo_copies(3, mid(xpf, 1), mid(xpf, depth))
    halo_start(pf_halo)
    parts["a2"].wait()
    a_halo = halo_copies(
        4, a_in.at[0, 0, :, :, pl.ds(half, half)], a_in.at[0, depth - 1, :, :, pl.ds(half, half)]
    )
    halo_start(a_halo)
    wgrad(xr, pf_s, 0)
    f1 = level_1(0)
    each(lambda z: fill(xa, z + 1, step, block(a_in, z, 1, 0)))
    halo_finish(a_halo, 4, xa)
    parts["a1"].wait()
    f2 = level_2(0, f1)

    def forward_one(z):
        b1 = block(a_in, z, 0, 0) + jnp.tanh(conv(xa, flat(w, 0, 0), z))
        put(fwd, z, 0, b1)
        fill(xb, z + 1, step, b1)

    each(forward_one)
    b_halo = halo_copies(5, mid(xb, 1), mid(xb, depth))
    halo_start(b_halo)
    g3 = level_3(1, g2)
    halo_finish(pf_halo, 3, xpf)
    each(lambda z: put(igrad, z, 1, block(c_in, z, 1, 0) + conv(xpf, flat(wt, 0), z)))
    f3 = level_3(0, f2)
    halo_finish(b_halo, 5, xb)
    each(
        lambda z: put(
            fwd, z, 1, block(a_in, z, 1, 0) + jnp.tanh(conv(xb, flat(w, 0, 1), z))
        )
    )
    g4 = level_4(1, g3)
    f4 = level_4(0, f3)
    g4.wait()
    gsum[1] = total[1]
    f4.wait()
    gsum[0] = total[0]


def shards(carried_act, stored_out, cotangent, weights, momentum):
    ns, nt = lax.axis_size("section"), lax.axis_size("tile")
    _, depth, hy, wx, chans = stored_out.shape
    half = chans // 2
    per = nt // 8
    tp = -(-27 // per)
    m = nt // 2
    step = 2 if depth % 2 == 0 else 1
    field = (depth + 2, hy + 2, wx, 3 * half)
    sems = 12 + 4 + 2 * (2 + 2 * (m - 1))
    vm = pltpu.VMEM
    cells = depth * hy * wx
    flops = 16 * cells * 27 * half * half
    fwd, igrad, gsum = pl.pallas_call(
        functools.partial(kernel, ns, nt, tp, step),
        out_shape=(
            jax.ShapeDtypeStruct((depth, hy, wx, chans), BF),
            jax.ShapeDtypeStruct((depth, hy, wx, chans), BF),
            jax.ShapeDtypeStruct((2, m, 2, tp, 16, half), BF),
        ),
        in_specs=[
            pl.BlockSpec(memory_space=pl.ANY),
            pl.BlockSpec(memory_space=vm),
            pl.BlockSpec(memory_space=pl.ANY),
            pl.BlockSpec(memory_space=vm),
        ],
        out_specs=[pl.BlockSpec(memory_space=vm)] * 3,
        scratch_shapes=[vm(field, BF)] * 6
        + [
            vm((6, 2, hy, wx, half), BF),
            vm((1, depth, hy, wx, chans), BF),
            vm((1, depth, hy, wx, chans), BF),
            vm((depth, hy * wx, half), F32),
            vm((depth, hy * wx, half), F32),
            vm((2, 27, half, half), BF),
            vm((depth, hy * wx, half), BF),
            vm((depth, hy * wx, half), BF),
            vm((2, m, 2, tp, 16, half), BF),
            vm((2, m, tp, 16, half), BF),
            vm((2, m, tp, 16, half), BF),
            vm((2, m - 1, tp, 16, half), BF),
            vm((2, m, 2, tp, 16, half), BF),
            pltpu.SemaphoreType.DMA((sems,)),
            pltpu.SemaphoreType.DMA((sems,)),
        ],
        compiler_params=pltpu.CompilerParams(
            collective_id=0, has_side_effects=True, vmem_limit_bytes=56 * 1024 * 1024
        ),
        cost_estimate=pl.CostEstimate(
            flops=flops, bytes_accessed=12 * 1024 * 1024, transcendentals=4 * cells * half
        ),
    )(carried_act, stored_out, cotangent, weights)
    count = depth * nt * hy * wx
    scale = grad_weight / jnp.sqrt(jnp.float32(count))
    grads = gsum.reshape(2, 8, per * tp, 16, half)[:, :, :27]
    grads = jnp.transpose(grads, (0, 2, 1, 3, 4)).reshape(momentum.shape)
    new_momentum = momentum_decay * momentum + grads.astype(F32) * scale
    return (fwd[None], igrad[None], new_momentum)


def solution(mesh):
    field = P("section", "tile", None, None, None)
    held = P("section", None, None, None, None)
    return jax.shard_map(
        shards,
        mesh=mesh,
        in_specs=(field, field, field, held, held),
        out_specs=(field, field, held),
        check_vma=False,
    )
```

profile of v0, /device:TPU:0, one launch (start us, length us, event | category | flops | bytes accessed | tf_op | source)
XLA Modules:
  0.0 85.2 jit_solution(15696650560201153636)
XLA Ops:
  0.6 76.3 %shard_map.76 = (bf16[6,16,16,256]{3,2,1,0:T(8,128)(2,1)}, bf16[6,16,16,256]{3,2,1,0:T(8,128)(2,1)}, bf16[2,4,2,27,16,128]{5,4,3,2,1,0:T(8,128)(2,1)}) custom-call(bf16[1,6,16,16,256]{4,3,2,1,0:T(8,128)(2,1)} %act.1, bf16[1,6,16,16,256]{4,3,2,1,0:T(8,128)(2,1)} %stored.1, bf16[1,6,16,16,256]{4,3,2,1,0:T(8,128)(2,1)} %cot.1, bf16[1,2,27,128,128]{4,3,2,1,0:T(8,128)(2,1)} %w.1), custom_call_target="tpu_custom_call" | custom-call | flops 10871635968 | bytes 12582912 | tf_op jit(solution)/shard_map/pallas_call | solution.py:331
  76.9 1.9 %convert_multiply_fusion = f32[2,4,2,27,16,128]{5,4,3,2,1,0:T(8,128)S(1)} fusion(bf16[2,4,2,27,16,128]{5,4,3,2,1,0:T(8,128)(2,1)} %get-tuple-element.8), kind=kLoop, calls=%fused_computation | loop fusion | flops 1769472 | bytes 5308416 | tf_op jit(solution)/shard_map/mul | solution.py:374
  78.8 0.0 copy-start
  78.8 0.5 copy.8
  79.3 1.5 %copy-done = f32[1,2,27,128,128]{4,3,2,1,0:T(8,128)S(1)} copy-done((f32[1,2,27,128,128]{4,3,2,1,0:T(8,128)S(1)}, f32[1,2,27,128,128]{4,3,2,1,0:T(8,128)}, u32[]{:S(2)}) %copy-start) | copy-done | bytes 3538968
  80.8 0.0 copy-start.2
  80.8 0.0 copy-start.1
  80.8 2.6 %multiply_add_fusion = f32[1,2,27,128,128]{4,3,2,1,0:T(8,128)} fusion(f32[1,2,27,128,128]{4,3,2,1,0:T(8,128)S(1)} %bitcast.7, f32[1,2,27,128,128]{4,3,2,1,0:T(8,128)S(1)} %copy-done), kind=kLoop, calls=%fused_computation.1 | loop fusion | flops 1769472 | bytes 10616832 | tf_op jit(solution)/shard_map/add | solution.py:374
  83.4 0.0 copy-done.2
  83.4 0.9 %copy.11 = bf16[1,6,16,16,256]{4,3,2,1,0:T(8,128)(2,1)} copy(bf16[1,6,16,16,256]{4,3,2,1,0:T(8,128)(2,1)S(1)} %bitcast.9) | data formatting | bytes 1572864
  84.3 0.0 copy-done.1
  84.3 0.9 %copy.12 = bf16[1,6,16,16,256]{4,3,2,1,0:T(8,128)(2,1)} copy(bf16[1,6,16,16,256]{4,3,2,1,0:T(8,128)(2,1)S(1)} %bitcast.8) | data formatting | bytes 1572864
Async XLA Ops:
  78.8 2.0 %copy-start = (f32[1,2,27,128,128]{4,3,2,1,0:T(8,128)S(1)}, f32[1,2,27,128,128]{4,3,2,1,0:T(8,128)}, u32[]{:S(2)}) copy-start(f32[1,2,27,128,128]{4,3,2,1,0:T(8,128)} %param.9) | copy-start | bytes 10616836
  80.8 2.6 %copy-start.2 = (bf16[6,16,16,256]{3,2,1,0:T(8,128)(2,1)S(1)}, bf16[6,16,16,256]{3,2,1,0:T(8,128)(2,1)}, u32[]{:S(2)}) copy-start(bf16[6,16,16,256]{3,2,1,0:T(8,128)(2,1)} %get-tuple-element.6) | copy-start | bytes 2359300
  80.8 3.5 %copy-start.1 = (bf16[6,16,16,256]{3,2,1,0:T(8,128)(2,1)S(1)}, bf16[6,16,16,256]{3,2,1,0:T(8,128)(2,1)}, u32[]{:S(2)}) copy-start(bf16[6,16,16,256]{3,2,1,0:T(8,128)(2,1)} %get-tuple-element.7) | copy-start | bytes 2359300
where the time goes:
time: 85.4 us; the launch traced here: 85.2 us
  Pallas kernels  76.3 us (89%)
  other arithmetic  4.46 us (5%)
  local copies, waits for them, and re-layouts  3.75 us (4%)
    pallas_call x1, Pallas kernels, shards(): pl.pallas_call(functools.partial(kernel, ns, nt, tp, step), out_shape=(ja...  76.3 us
    unnamed x8, local copies, waits for them, and re-layouts  3.27 us
    add x1, other arithmetic, shards(): new_momentum = momentum_decay * momentum + grads.astype(F32) * scale  2.57 us
    mul x1, other arithmetic, shards(): new_momentum = momentum_decay * momentum + grads.astype(F32) * scale  1.89 us

commit v1 on v0

--- a/solution.py
+++ b/solution.py
@@ -157,8 +157,8 @@
     ):
         view = (0, slice(None), slice(None), slice(None), pl.ds(piece * half, half))
         parts[name] = copy(src.at[view], dst.at[view], target, t)
-        parts[name].start()
-
+
+    parts["c2"].start()
     for x in (xz, xr, xpg, xpf, xa, xb):
         clear(x)
     each(lambda z: fill(xz, z + 1, step, block(stored, z, 0, 0)))
@@ -182,7 +182,9 @@
     each(reconstruct)
     r_halo = halo_copies(1, mid(xr, 1), mid(xr, depth))
     halo_start(r_halo)
-    parts["c2"].wait()
+    parts["c2"].wait_send()
+    parts["c1"].start()
+    parts["c2"].wait_recv()
 
     def pre_g(z):
         v = block(c_in, z, 1, 0) * gz_s[pl.ds(z, step)].reshape(rows, half)
@@ -265,7 +267,9 @@
     each(recompute_f)
     g2 = level_2(1, g1)
     halo_finish(pg_halo, 2, xpg)
-    parts["c1"].wait()
+    parts["c1"].wait_send()
+    parts["a2"].start()
+    parts["c1"].wait_recv()
 
     def grad_one(z):
         d1 = (block(c_in, z, 0, 0) + conv(xpg, flat(wt, 1), z)).astype(BF)
@@ -277,42 +281,58 @@
     each(grad_one)
     pf_halo = halo_copies(3, mid(xpf, 1), mid(xpf, depth))
     halo_start(pf_halo)
-    parts["a2"].wait()
+    wgrad(xr, pf_s, 0)
+    f1 = level_1(0)
+    parts["a2"].wait_send()
+    parts["a1"].start()
+    g3 = level_3(1, g2)
+    halo_finish(pf_halo, 3, xpf)
+    each(lambda z: put(igrad, z, 1, block(c_in, z, 1, 0) + conv(xpf, flat(wt, 0), z)))
+    f2 = level_2(0, f1)
+    parts["a2"].wait_recv()
     a_halo = halo_copies(
         4, a_in.at[0, 0, :, :, pl.ds(half, half)], a_in.at[0, depth - 1, :, :, pl.ds(half, half)]
     )
     halo_start(a_halo)
-    wgrad(xr, pf_s, 0)
-    f1 = level_1(0)
     each(lambda z: fill(xa, z + 1, step, block(a_in, z, 1, 0)))
     halo_finish(a_halo, 4, xa)
+
+    def forward_conv(z):
+        gz_s[pl.ds(z, step)] = jnp.tanh(conv(xa, flat(w, 0, 0), z)).reshape(step, plane, half)
+
+    each(forward_conv)
     parts["a1"].wait()
-    f2 = level_2(0, f1)
 
     def forward_one(z):
-        b1 = block(a_in, z, 0, 0) + jnp.tanh(conv(xa, flat(w, 0, 0), z))
+        b1 = block(a_in, z, 0, 0) + gz_s[pl.ds(z, step)].reshape(rows, half)
         put(fwd, z, 0, b1)
         fill(xb, z + 1, step, b1)
 
     each(forward_one)
     b_halo = halo_copies(5, mid(xb, 1), mid(xb, depth))
     halo_start(b_halo)
-    g3 = level_3(1, g2)
-    halo_finish(pf_halo, 3, xpf)
-    each(lambda z: put(igrad, z, 1, block(c_in, z, 1, 0) + conv(xpf, flat(wt, 0), z)))
     f3 = level_3(0, f2)
+    g4 = level_4(1, g3)
     halo_finish(b_halo, 5, xb)
     each(
         lambda z: put(
             fwd, z, 1, block(a_in, z, 1, 0) + jnp.tanh(conv(xb, flat(w, 0, 1), z))
         )
     )
-    g4 = level_4(1, g3)
-    f4 = level_4(0, f3)
+
+    def lay_out(g):
+        per = nt // 8
+        for share in range(nt):
+            r, first = share // per, (share % per) * tp
+            count = min(27 - first, tp)
+            gsum[g, pl.ds(first, count), pl.ds(16 * r, 16)] = total[
+                g, share // 2, share % 2, pl.ds(0, count)
+            ]
+
     g4.wait()
-    gsum[1] = total[1]
-    f4.wait()
-    gsum[0] = total[0]
+    lay_out(1)
+    level_4(0, f3).wait()
+    lay_out(0)
 
 
 def shards(carried_act, stored_out, cotangent, weights, momentum):
@@ -333,7 +353,7 @@
         out_shape=(
             jax.ShapeDtypeStruct((depth, hy, wx, chans), BF),
             jax.ShapeDtypeStruct((depth, hy, wx, chans), BF),
-            jax.ShapeDtypeStruct((2, m, 2, tp, 16, half), BF),
+            jax.ShapeDtypeStruct((2, 27, half, half), BF),
         ),
         in_specs=[
             pl.BlockSpec(memory_space=pl.ANY),
@@ -369,9 +389,7 @@
     )(carried_act, stored_out, cotangent, weights)
     count = depth * nt * hy * wx
     scale = grad_weight / jnp.sqrt(jnp.float32(count))
-    grads = gsum.reshape(2, 8, per * tp, 16, half)[:, :, :27]
-    grads = jnp.transpose(grads, (0, 2, 1, 3, 4)).reshape(momentum.shape)
-    new_momentum = momentum_decay * momentum + grads.astype(F32) * scale
+    new_momentum = momentum_decay * momentum + gsum[None].astype(F32) * scale
     return (fwd[None], igrad[None], new_momentum)
 
 

time: 85.4 us -> 75.3 us (0.88)
  the two profiles are of different devices: /device:TPU:0 before, /device:TPU:11 now
where the time goes in v1:
time: 75.3 us; the launch traced here: 75.2 us
  Pallas kernels  68.5 us (91%)
  other arithmetic  4.2 us (6%)
  local copies, waits for them, and re-layouts  1.77 us (2%)
    pallas_call x1, Pallas kernels, shards(): pl.pallas_call(functools.partial(kernel, ns, nt, tp, step), out_shape=(ja...  68.5 us
    add x1, other arithmetic, shards(): new_momentum = momentum_decay * momentum + gsum[None].astype(F32) * scale  4.2 us
    unnamed x8, local copies, waits for them, and re-layouts  1.77 us

profile of v1, /device:TPU:11, one launch (start us, length us, event | category | flops | bytes accessed | tf_op | source)
XLA Modules:
  0.0 75.2 jit_solution(11731211075690351396)
XLA Ops:
  0.6 0.0 copy-start
  0.6 68.5 %shard_map.76 = (bf16[6,16,16,256]{3,2,1,0:T(8,128)(2,1)}, bf16[6,16,16,256]{3,2,1,0:T(8,128)(2,1)}, bf16[2,27,128,128]{3,2,1,0:T(8,128)(2,1)}) custom-call(bf16[1,6,16,16,256]{4,3,2,1,0:T(8,128)(2,1)} %act.1, bf16[1,6,16,16,256]{4,3,2,1,0:T(8,128)(2,1)} %stored.1, bf16[1,6,16,16,256]{4,3,2,1,0:T(8,128)(2,1)} %cot.1, bf16[1,2,27,128,128]{4,3,2,1,0:T(8,128)(2,1)} %w.1), custom_call_target="tpu_custom_call" | custom-call | flops 10871635968 | bytes 12582912 | tf_op jit(solution)/shard_map/pallas_call | solution.py:351
  69.2 0.0 copy-done
  69.2 0.0 copy-start.2
  69.2 0.0 copy-start.1
  69.2 4.2 %bitcast_add_fusion = f32[1,2,27,128,128]{4,3,2,1,0:T(8,128)} fusion(bf16[2,27,128,128]{3,2,1,0:T(8,128)(2,1)} %get-tuple-element.8, f32[1,2,27,128,128]{4,3,2,1,0:T(8,128)S(1)} %copy-done), kind=kLoop, calls=%fused_computation | loop fusion | flops 3538944 | bytes 8847360 | tf_op jit(solution)/shard_map/add | solution.py:392
  73.4 0.0 copy-done.2
  73.4 0.9 %copy.10 = bf16[1,6,16,16,256]{4,3,2,1,0:T(8,128)(2,1)} copy(bf16[1,6,16,16,256]{4,3,2,1,0:T(8,128)(2,1)S(1)} %bitcast.5) | data formatting | bytes 1572864
  74.3 0.0 copy-done.1
  74.3 0.9 %copy.11 = bf16[1,6,16,16,256]{4,3,2,1,0:T(8,128)(2,1)} copy(bf16[1,6,16,16,256]{4,3,2,1,0:T(8,128)(2,1)S(1)} %bitcast.4) | data formatting | bytes 1572864
Async XLA Ops:
  0.6 68.5 %copy-start = (f32[1,2,27,128,128]{4,3,2,1,0:T(8,128)S(1)}, f32[1,2,27,128,128]{4,3,2,1,0:T(8,128)}, u32[]{:S(2)}) copy-start(f32[1,2,27,128,128]{4,3,2,1,0:T(8,128)} %param.9) | copy-start | bytes 10616836
  69.2 4.2 %copy-start.2 = (bf16[6,16,16,256]{3,2,1,0:T(8,128)(2,1)S(1)}, bf16[6,16,16,256]{3,2,1,0:T(8,128)(2,1)}, u32[]{:S(2)}) copy-start(bf16[6,16,16,256]{3,2,1,0:T(8,128)(2,1)} %get-tuple-element.6) | copy-start | bytes 2359300
  69.2 5.1 %copy-start.1 = (bf16[6,16,16,256]{3,2,1,0:T(8,128)(2,1)S(1)}, bf16[6,16,16,256]{3,2,1,0:T(8,128)(2,1)}, u32[]{:S(2)}) copy-start(bf16[6,16,16,256]{3,2,1,0:T(8,128)(2,1)} %get-tuple-element.7) | copy-start | bytes 2359300

commit v2 on v1

--- a/solution.py
+++ b/solution.py
@@ -168,7 +168,6 @@
             wt[which, n] = w[0, which, 26 - n].T
         return carry
 
-    lax.fori_loop(0, 27, turn, 0)
     halo_finish(z_halo, 0, xz)
 
     def flat(ref, *lead):
@@ -184,6 +183,7 @@
     halo_start(r_halo)
     parts["c2"].wait_send()
     parts["c1"].start()
+    lax.fori_loop(0, 27, turn, 0)
     parts["c2"].wait_recv()
 
     def pre_g(z):
@@ -287,8 +287,9 @@
     parts["a1"].start()
     g3 = level_3(1, g2)
     halo_finish(pf_halo, 3, xpf)
+    f2 = level_2(0, f1)
     each(lambda z: put(igrad, z, 1, block(c_in, z, 1, 0) + conv(xpf, flat(wt, 0), z)))
-    f2 = level_2(0, f1)
+    g4 = level_4(1, g3)
     parts["a2"].wait_recv()
     a_halo = halo_copies(
         4, a_in.at[0, 0, :, :, pl.ds(half, half)], a_in.at[0, depth - 1, :, :, pl.ds(half, half)]
@@ -301,6 +302,7 @@
         gz_s[pl.ds(z, step)] = jnp.tanh(conv(xa, flat(w, 0, 0), z)).reshape(step, plane, half)
 
     each(forward_conv)
+    f3 = level_3(0, f2)
     parts["a1"].wait()
 
     def forward_one(z):
@@ -311,8 +313,6 @@
     each(forward_one)
     b_halo = halo_copies(5, mid(xb, 1), mid(xb, depth))
     halo_start(b_halo)
-    f3 = level_3(0, f2)
-    g4 = level_4(1, g3)
     halo_finish(b_halo, 5, xb)
     each(
         lambda z: put(
@@ -342,7 +342,7 @@
     per = nt // 8
     tp = -(-27 // per)
     m = nt // 2
-    step = 2 if depth % 2 == 0 else 1
+    step = 3 if depth % 3 == 0 else 1
     field = (depth + 2, hy + 2, wx, 3 * half)
     sems = 12 + 4 + 2 * (2 + 2 * (m - 1))
     vm = pltpu.VMEM

time: 75.3 us -> 80.2 us (1.065)
  Pallas kernels: 68.5 us -> 73.4 us
    pallas_call x1, Pallas kernels: 68.5 us -> 73.4 us  [shards(): pl.pallas_call(functools.partial(kernel, ns, nt, tp, step), out_shape=(ja...]
where the time goes in v2:
time: 80.2 us; the launch traced here: 80 us
  Pallas kernels  73.4 us (92%)
  other arithmetic  4.2 us (5%)
  local copies, waits for them, and re-layouts  1.77 us (2%)
    pallas_call x1, Pallas kernels, shards(): pl.pallas_call(functools.partial(kernel, ns, nt, tp, step), out_shape=(ja...  73.4 us
    add x1, other arithmetic, shards(): new_momentum = momentum_decay * momentum + gsum[None].astype(F32) * scale  4.2 us
    unnamed x8, local copies, waits for them, and re-layouts  1.77 us

profile of v2, /device:TPU:11, one launch (start us, length us, event | category | flops | bytes accessed | tf_op | source)
XLA Modules:
  0.0 80.0 jit_solution(5559096162471037432)
XLA Ops:
  0.6 0.0 copy-start
  0.6 73.4 %shard_map.76 = (bf16[6,16,16,256]{3,2,1,0:T(8,128)(2,1)}, bf16[6,16,16,256]{3,2,1,0:T(8,128)(2,1)}, bf16[2,27,128,128]{3,2,1,0:T(8,128)(2,1)}) custom-call(bf16[1,6,16,16,256]{4,3,2,1,0:T(8,128)(2,1)} %act.1, bf16[1,6,16,16,256]{4,3,2,1,0:T(8,128)(2,1)} %stored.1, bf16[1,6,16,16,256]{4,3,2,1,0:T(8,128)(2,1)} %cot.1, bf16[1,2,27,128,128]{4,3,2,1,0:T(8,128)(2,1)} %w.1), custom_call_target="tpu_custom_call" | custom-call | flops 10871635968 | bytes 12582912 | tf_op jit(solution)/shard_map/pallas_call | solution.py:351
  74.0 0.0 copy-done
  74.0 0.0 copy-start.2
  74.0 0.0 copy-start.1
  74.0 4.2 %bitcast_add_fusion = f32[1,2,27,128,128]{4,3,2,1,0:T(8,128)} fusion(bf16[2,27,128,128]{3,2,1,0:T(8,128)(2,1)} %get-tuple-element.8, f32[1,2,27,128,128]{4,3,2,1,0:T(8,128)S(1)} %copy-done), kind=kLoop, calls=%fused_computation | loop fusion | flops 3538944 | bytes 8847360 | tf_op jit(solution)/shard_map/add | solution.py:392
  78.2 0.0 copy-done.2
  78.2 0.9 %copy.10 = bf16[1,6,16,16,256]{4,3,2,1,0:T(8,128)(2,1)} copy(bf16[1,6,16,16,256]{4,3,2,1,0:T(8,128)(2,1)S(1)} %bitcast.5) | data formatting | bytes 1572864
  79.1 0.0 copy-done.1
  79.1 0.9 %copy.11 = bf16[1,6,16,16,256]{4,3,2,1,0:T(8,128)(2,1)} copy(bf16[1,6,16,16,256]{4,3,2,1,0:T(8,128)(2,1)S(1)} %bitcast.4) | data formatting | bytes 1572864
Async XLA Ops:
  0.6 73.4 %copy-start = (f32[1,2,27,128,128]{4,3,2,1,0:T(8,128)S(1)}, f32[1,2,27,128,128]{4,3,2,1,0:T(8,128)}, u32[]{:S(2)}) copy-start(f32[1,2,27,128,128]{4,3,2,1,0:T(8,128)} %param.9) | copy-start | bytes 10616836
  74.0 4.2 %copy-start.2 = (bf16[6,16,16,256]{3,2,1,0:T(8,128)(2,1)S(1)}, bf16[6,16,16,256]{3,2,1,0:T(8,128)(2,1)}, u32[]{:S(2)}) copy-start(bf16[6,16,16,256]{3,2,1,0:T(8,128)(2,1)} %get-tuple-element.6) | copy-start | bytes 2359300
  74.0 5.1 %copy-start.1 = (bf16[6,16,16,256]{3,2,1,0:T(8,128)(2,1)S(1)}, bf16[6,16,16,256]{3,2,1,0:T(8,128)(2,1)}, u32[]{:S(2)}) copy-start(bf16[6,16,16,256]{3,2,1,0:T(8,128)(2,1)} %get-tuple-element.7) | copy-start | bytes 2359300

commit v3 on v1

--- a/solution.py
+++ b/solution.py
@@ -168,7 +168,6 @@
             wt[which, n] = w[0, which, 26 - n].T
         return carry
 
-    lax.fori_loop(0, 27, turn, 0)
     halo_finish(z_halo, 0, xz)
 
     def flat(ref, *lead):
@@ -184,6 +183,7 @@
     halo_start(r_halo)
     parts["c2"].wait_send()
     parts["c1"].start()
+    lax.fori_loop(0, 27, turn, 0)
     parts["c2"].wait_recv()
 
     def pre_g(z):
@@ -342,7 +342,7 @@
     per = nt // 8
     tp = -(-27 // per)
     m = nt // 2
-    step = 2 if depth % 2 == 0 else 1
+    step = 1
     field = (depth + 2, hy + 2, wx, 3 * half)
     sems = 12 + 4 + 2 * (2 + 2 * (m - 1))
     vm = pltpu.VMEM

time: 75.3 us -> 77.1 us (1.024)
  Pallas kernels: 68.5 us -> 69.9 us
    pallas_call x1, Pallas kernels: 68.5 us -> 69.9 us  [shards(): pl.pallas_call(functools.partial(kernel, ns, nt, tp, step), out_shape=(ja...]
where the time goes in v3:
time: 77.1 us; the launch traced here: 76.6 us
  Pallas kernels  69.9 us (91%)
  other arithmetic  4.2 us (5%)
  local copies, waits for them, and re-layouts  1.77 us (2%)
    pallas_call x1, Pallas kernels, shards(): pl.pallas_call(functools.partial(kernel, ns, nt, tp, step), out_shape=(ja...  69.9 us
    add x1, other arithmetic, shards(): new_momentum = momentum_decay * momentum + gsum[None].astype(F32) * scale  4.2 us
    unnamed x8, local copies, waits for them, and re-layouts  1.77 us

profile of v3, /device:TPU:11, one launch (start us, length us, event | category | flops | bytes accessed | tf_op | source)
XLA Modules:
  0.0 76.6 jit_solution(11819811848363961549)
XLA Ops:
  0.6 0.0 copy-start
  0.6 69.9 %shard_map.76 = (bf16[6,16,16,256]{3,2,1,0:T(8,128)(2,1)}, bf16[6,16,16,256]{3,2,1,0:T(8,128)(2,1)}, bf16[2,27,128,128]{3,2,1,0:T(8,128)(2,1)}) custom-call(bf16[1,6,16,16,256]{4,3,2,1,0:T(8,128)(2,1)} %act.1, bf16[1,6,16,16,256]{4,3,2,1,0:T(8,128)(2,1)} %stored.1, bf16[1,6,16,16,256]{4,3,2,1,0:T(8,128)(2,1)} %cot.1, bf16[1,2,27,128,128]{4,3,2,1,0:T(8,128)(2,1)} %w.1), custom_call_target="tpu_custom_call" | custom-call | flops 10871635968 | bytes 12582912 | tf_op jit(solution)/shard_map/pallas_call | solution.py:351
  70.6 0.0 copy-done
  70.6 0.0 copy-start.2
  70.6 0.0 copy-start.1
  70.6 4.2 %bitcast_add_fusion = f32[1,2,27,128,128]{4,3,2,1,0:T(8,128)} fusion(bf16[2,27,128,128]{3,2,1,0:T(8,128)(2,1)} %get-tuple-element.8, f32[1,2,27,128,128]{4,3,2,1,0:T(8,128)S(1)} %copy-done), kind=kLoop, calls=%fused_computation | loop fusion | flops 3538944 | bytes 8847360 | tf_op jit(solution)/shard_map/add | solution.py:392
  74.8 0.0 copy-done.2
  74.8 0.9 %copy.10 = bf16[1,6,16,16,256]{4,3,2,1,0:T(8,128)(2,1)} copy(bf16[1,6,16,16,256]{4,3,2,1,0:T(8,128)(2,1)S(1)} %bitcast.5) | data formatting | bytes 1572864
  75.7 0.0 copy-done.1
  75.7 0.9 %copy.11 = bf16[1,6,16,16,256]{4,3,2,1,0:T(8,128)(2,1)} copy(bf16[1,6,16,16,256]{4,3,2,1,0:T(8,128)(2,1)S(1)} %bitcast.4) | data formatting | bytes 1572864
Async XLA Ops:
  0.6 69.9 %copy-start = (f32[1,2,27,128,128]{4,3,2,1,0:T(8,128)S(1)}, f32[1,2,27,128,128]{4,3,2,1,0:T(8,128)}, u32[]{:S(2)}) copy-start(f32[1,2,27,128,128]{4,3,2,1,0:T(8,128)} %param.9) | copy-start | bytes 10616836
  70.6 4.2 %copy-start.2 = (bf16[6,16,16,256]{3,2,1,0:T(8,128)(2,1)S(1)}, bf16[6,16,16,256]{3,2,1,0:T(8,128)(2,1)}, u32[]{:S(2)}) copy-start(bf16[6,16,16,256]{3,2,1,0:T(8,128)(2,1)} %get-tuple-element.6) | copy-start | bytes 2359300
  70.6 5.1 %copy-start.1 = (bf16[6,16,16,256]{3,2,1,0:T(8,128)(2,1)S(1)}, bf16[6,16,16,256]{3,2,1,0:T(8,128)(2,1)}, u32[]{:S(2)}) copy-start(bf16[6,16,16,256]{3,2,1,0:T(8,128)(2,1)} %get-tuple-element.7) | copy-start | bytes 2359300
